TPU v7x, 32 devices: a whole 2x2x4 slice. The times are simulated.
32 devices in a mesh: groups: 2 (over x), inst: 16 (over z, y, core).
Axes of the slice: x: 2, y: 2, z: 4, core: 2. Of those that a mesh axis runs over, the one named last changes fastest.
Arguments:
- queries: bfloat16 [4096, 8192], P(('groups', 'inst')), parts along dimension 0, may hold values from -128 to 128
- span_kv: bfloat16 [4096, 2048], P(('groups', 'inst')), parts along dimension 0, may hold values from -6 to 6
- prefix_kv: bfloat16 [32768, 2048], P(('groups', 'inst')), parts along dimension 0, may hold values from -6 to 6
- span_counts: int32 [32], P('groups'), parts along dimension 0, may hold values from 1 to 128, 1536 in all
- prefix_lengths: int32 [32], P('groups'), parts along dimension 0, may hold values from 1 to 1024, 10240 in all
- move_to: int32 [32], P('groups'), parts along dimension 0, may hold values from 0 to 15, each once
- page_slot: int32 [256], P('groups'), parts along dimension 0, may hold values from 0 to 127, each once
Outputs:
- attn_out: bfloat16 [4096, 8192], P(('groups', 'inst')), parts along dimension 0
- decode_pages: bfloat16 [256, 16, 2048], P(('groups', 'inst')), parts along dimension 0
There are 2 independent parts, one for each index of `groups`. A program takes and returns all parts, laid end to end along the dimension named above; each array names one. Nothing has to cross between parts.
Inputs may be any that keep to these rules, and one draw needn't show every extreme that they name: `move_to`: each instance's span result goes to exactly one instance, and each instance receives exactly one. `page_slot`: each decode slot receives exactly one page.
All inputs are finite; a program needn't handle non-finite values.
Results may differ from a plain program's by a relative error of at most 0.0049.
Values may be sent and summed in bfloat16 or wider, within the bound.
A program may use at most 64 MiB of HBM per device.

v0:
```python
import functools
import math

import jax
import jax.numpy as jnp
from jax import lax
from jax.experimental import pallas as pl
from jax.experimental.pallas import tpu as pltpu
from jax.sharding import PartitionSpec as P

HEADS = 64
KV_HEADS = 8
HEAD_DIM = 128
PAGE = 16
KEY_WIDTH = KV_HEADS * HEAD_DIM
GROUP_WIDTH = HEADS // KV_HEADS * HEAD_DIM
ROWS = 16
COLS = 512
MESH = pl.DeviceIdType.MESH


def kernel(n, with_pages, *refs):
    if with_pages:
        (counts, lengths, source_of, page_source, q_hbm, span_hbm, prefix_hbm, new_hbm,
         out_hbm, pages_hbm, q, kv, bias, stage, relay, *rest) = refs
        chunks = 128 // n
        held = rest[:chunks]
        (page_stage, page_held, q_sem, k_sem, v_sem, span_sem, send_sem, held_sem, relay_sem,
         out_sem, page_sem) = rest[chunks:]
    else:
        (counts, lengths, source_of, q_hbm, span_hbm, prefix_hbm,
         out_hbm, q, kv, bias, stage, relay, *rest) = refs
        chunks = 128 // n
        held = rest[:chunks]
        q_sem, k_sem, v_sem, span_sem, send_sem, held_sem, relay_sem, out_sem = rest[chunks:]
    me = lax.axis_index("inst")
    span = span_hbm.shape[0]
    prefix = prefix_hbm.shape[0]
    keys = prefix + span

    span_copies = [
        pltpu.make_async_copy(span_hbm, kv.at[pl.ds(prefix, span)], span_sem)
    ]
    loads = []
    for g in range(KV_HEADS):
        wide = pl.ds(g * GROUP_WIDTH, GROUP_WIDTH)
        k_cols = pl.ds(g * HEAD_DIM, HEAD_DIM)
        v_cols = pl.ds(KEY_WIDTH + g * HEAD_DIM, HEAD_DIM)
        loads.append([
            pltpu.make_async_copy(q_hbm.at[:, wide], q.at[:, wide], q_sem.at[g]),
            pltpu.make_async_copy(
                prefix_hbm.at[:, k_cols], kv.at[pl.ds(0, prefix), k_cols], k_sem.at[g]),
            pltpu.make_async_copy(
                prefix_hbm.at[:, v_cols], kv.at[pl.ds(0, prefix), v_cols], v_sem.at[g]),
        ])
    span_copies[0].start()
    for group in loads:
        for copy in group:
            copy.start()

    barrier = pltpu.get_barrier_semaphore()

    @pl.loop(1, n)
    def _(k):
        pl.semaphore_signal(
            barrier, inc=1, device_id={"inst": lax.rem(me + k, n)}, device_id_type=MESH)

    count = counts[me]
    length = lengths[me]
    row = lax.broadcasted_iota(jnp.int32, (span, keys), 0)
    column = lax.broadcasted_iota(jnp.int32, (span, keys), 1)
    limit = jnp.where(column < prefix, length, row + (prefix + 1))
    bias[...] = jnp.where(column < limit, 0.0, -1e30)
    pl.semaphore_wait(barrier, n - 1)

    if with_pages:
        pages_dev = span // PAGE

        @pl.loop(1, n)
        def _(k):
            peer = lax.rem(me + k, n)
            pltpu.make_async_remote_copy(
                src_ref=new_hbm.at[:, :, pl.ds(pl.multiple_of(peer * 128, 128), 128)],
                dst_ref=page_held.at[pl.ds(me * pages_dev, pages_dev)],
                send_sem=page_sem.at[0],
                recv_sem=page_sem.at[1],
                device_id={"inst": peer},
                device_id_type=MESH,
            ).start()

        pltpu.make_async_copy(
            new_hbm.at[:, :, pl.ds(pl.multiple_of(me * 128, 128), 128)],
            page_held.at[pl.ds(me * pages_dev, pages_dev)],
            page_sem.at[1],
        ).start()

    scale = math.log2(math.e) / math.sqrt(HEAD_DIM)
    live = lax.broadcasted_iota(jnp.int32, (span, HEAD_DIM), 0) < count

    def attend(g):
        @pl.loop(0, 4)
        def _(pair):
            first = pl.multiple_of(g * GROUP_WIDTH + pair * 256, 256)
            two = q[:, pl.ds(first, 256)]
            rows = jnp.concatenate([two[:, :HEAD_DIM], two[:, HEAD_DIM:]], axis=0)
            key = kv[:, g * HEAD_DIM:(g + 1) * HEAD_DIM]
            value = kv[:, KEY_WIDTH + g * HEAD_DIM:KEY_WIDTH + (g + 1) * HEAD_DIM]
            scores = lax.dot_general(
                rows, key, (((1,), (1,)), ((), ())), preferred_element_type=jnp.float32)
            scores = scores.reshape(2, span, keys) * scale + bias[...][None]
            top = jnp.max(scores, axis=2, keepdims=True)
            shifted = jnp.exp2(scores - top)
            total = jnp.sum(shifted, axis=2, keepdims=True)
            mixed = jnp.dot(
                shifted.reshape(2 * span, keys).astype(jnp.bfloat16), value,
                preferred_element_type=jnp.float32)
            mixed = mixed.reshape(2, span, HEAD_DIM) / total
            mixed = jnp.where(live[None], mixed, 0.0).astype(jnp.bfloat16)
            half = pair // 2
            for h in range(2):
                at = pl.multiple_of((pair % 2) * 256 + h * HEAD_DIM, HEAD_DIM)
                for r in range(8):
                    stage[g, half * 8 + r, :, pl.ds(at, HEAD_DIM)] = (
                        mixed[h, r * ROWS:(r + 1) * ROWS])

    def spread(g):
        c = g * 16 // n

        @pl.loop(0, 16)
        def _(k):
            j = lax.rem(me + k, 16)
            target = (g * 16) % n + j

            @pl.when(target != me)
            def _():
                pltpu.make_async_remote_copy(
                    src_ref=stage.at[g, j],
                    dst_ref=held[c].at[me],
                    send_sem=send_sem.at[0],
                    recv_sem=held_sem.at[c],
                    device_id={"inst": target},
                    device_id_type=MESH,
                ).start()

            @pl.when(target == me)
            def _():
                pltpu.make_async_copy(stage.at[g, j], held[c].at[me], held_sem.at[c]).start()

    def send_on(c):
        pltpu.make_async_copy(held[c], held[c], held_sem.at[c]).wait()
        piece = c * n + me
        g = piece // 16
        j = piece % 16
        place = out_hbm.at[
            pl.ds(pl.multiple_of((j % 8) * ROWS, ROWS), ROWS),
            pl.ds(pl.multiple_of(g * GROUP_WIDTH + (j // 8) * COLS, COLS), COLS),
        ]

        @pl.loop(0, n)
        def _(k):
            peer = lax.rem(me + k, n)
            relay[c, peer] = held[c][source_of[peer]]

            @pl.when(k > 0)
            def _():
                pltpu.make_async_remote_copy(
                    src_ref=relay.at[c, peer],
                    dst_ref=place,
                    send_sem=relay_sem.at[0],
                    recv_sem=out_sem.at[0],
                    device_id={"inst": peer},
                    device_id_type=MESH,
                ).start()

            @pl.when(k == 0)
            def _():
                pltpu.make_async_copy(relay.at[c, peer], place, out_sem.at[0]).start()

    def send_pages():
        pltpu.make_async_copy(page_held, page_held, page_sem.at[1]).wait()
        place = pages_hbm.at[:, :, pl.ds(pl.multiple_of(me * 128, 128), 128)]

        @pl.loop(0, n)
        def _(k):
            peer = lax.rem(me + k, n)
            for slot in range(pages_dev):
                at = peer * pages_dev + slot
                page_stage[at] = page_held[page_source[at]]

            src = page_stage.at[pl.ds(peer * pages_dev, pages_dev)]

            @pl.when(k > 0)
            def _():
                pltpu.make_async_remote_copy(
                    src_ref=src,
                    dst_ref=place,
                    send_sem=page_sem.at[2],
                    recv_sem=page_sem.at[3],
                    device_id={"inst": peer},
                    device_id_type=MESH,
                ).start()

            @pl.when(k == 0)
            def _():
                pltpu.make_async_copy(src, place, page_sem.at[3]).start()

    lag = 3
    span_copies[0].wait()
    sent = 0
    for g in range(KV_HEADS):
        for copy in loads[g]:
            copy.wait()
        attend(g)
        spread(g)
        if with_pages and g == 3:
            send_pages()
        if n == 16 and g >= lag:
            send_on(sent)
            sent += 1
    for c in range(sent, chunks):
        send_on(c)

    away = 128 - chunks
    flat = stage.at[:, pl.ds(0, 15)]
    if n == 16:
        pltpu.make_async_copy(flat, flat, send_sem.at[0]).wait()
        flat = relay.at[:, pl.ds(0, n - 1)]
        pltpu.make_async_copy(flat, flat, relay_sem.at[0]).wait()
    else:
        flat = relay.at[0, pl.ds(0, away)]
        pltpu.make_async_copy(flat, flat, send_sem.at[0]).wait()
        pltpu.make_async_copy(flat, flat, relay_sem.at[0]).wait()
    pltpu.make_async_copy(out_hbm, out_hbm, out_sem.at[0]).wait()
    if with_pages:
        some = page_held.at[pl.ds(0, (n - 1) * pages_dev)]
        pltpu.make_async_copy(some, some, page_sem.at[0]).wait()
        some = page_stage.at[pl.ds(0, (n - 1) * pages_dev)]
        pltpu.make_async_copy(some, some, page_sem.at[2]).wait()
        pltpu.make_async_copy(pages_hbm, pages_hbm, page_sem.at[3]).wait()


def inverse(order):
    index = jnp.arange(order.shape[0], dtype=jnp.int32)
    return jnp.sum(jnp.where(order[None, :] == index[:, None], index[None, :], 0), axis=1)


def move_pages(span_kv, page_slot, inst_count):
    pages_here = span_kv.shape[0] // PAGE
    piece_width = PAGE * span_kv.shape[1] // inst_count
    flat_pages = span_kv.reshape(pages_here, inst_count, piece_width)
    spread_pages = lax.all_to_all(flat_pages, "inst", split_axis=1, concat_axis=0, tiled=True)
    ordered_pages = jnp.take(spread_pages, inverse(page_slot), axis=0)
    arrived = lax.all_to_all(ordered_pages, "inst", split_axis=0, concat_axis=1, tiled=True)
    return arrived.reshape(pages_here, PAGE, span_kv.shape[1])


def local(n, queries, span_kv, prefix_kv, span_counts, prefix_lengths, move_to, page_slot):
    span, width = queries.shape
    prefix, kv_width = prefix_kv.shape
    with_pages = n * 128 == kv_width
    chunks = 128 // n
    anywhere = pl.BlockSpec(memory_space=pl.ANY)
    scalars = pl.BlockSpec(memory_space=pltpu.SMEM)
    small = [span_counts, prefix_lengths, inverse(move_to)]
    out_shape = [jax.ShapeDtypeStruct((span, width), jnp.bfloat16)]
    scratch = [
        pltpu.VMEM((span, width), jnp.bfloat16),
        pltpu.VMEM((prefix + span, kv_width), jnp.bfloat16),
        pltpu.VMEM((span, prefix + span), jnp.float32),
        pltpu.VMEM((KV_HEADS, 16, ROWS, COLS), jnp.bfloat16),
        pltpu.VMEM((chunks, n, ROWS, COLS), jnp.bfloat16),
    ] + [pltpu.VMEM((n, ROWS, COLS), jnp.bfloat16) for _ in range(chunks)]
    big = [queries, span_kv, prefix_kv]
    if with_pages:
        small.append(inverse(page_slot))
        big.append(span_kv.reshape(span // PAGE, PAGE, kv_width))
        out_shape.append(jax.ShapeDtypeStruct((span // PAGE, PAGE, kv_width), jnp.bfloat16))
        scratch += [
            pltpu.VMEM((page_slot.shape[0], PAGE, 128), jnp.bfloat16),
            pltpu.VMEM((page_slot.shape[0], PAGE, 128), jnp.bfloat16),
        ]
    dma = pltpu.SemaphoreType.DMA
    scratch += [
        dma((KV_HEADS,)), dma((KV_HEADS,)), dma((KV_HEADS,)), dma(()),
        dma((1,)), dma((chunks,)), dma((1,)), dma((1,)),
    ]
    if with_pages:
        scratch.append(dma((4,)))
    outs = pl.pallas_call(
        functools.partial(kernel, n, with_pages),
        out_shape=out_shape,
        in_specs=[scalars] * len(small) + [anywhere] * len(big),
        out_specs=[anywhere] * len(out_shape),
        scratch_shapes=scratch,
        compiler_params=pltpu.CompilerParams(
            collective_id=0, has_side_effects=True, vmem_limit_bytes=48 * 1024 * 1024),
    )(*small, *big)
    if with_pages:
        return outs[0], outs[1]
    return outs[0], move_pages(span_kv, page_slot, n)


def solution(mesh):
    placed = (
        P(("groups", "inst"), None),
        P(("groups", "inst"), None),
        P(("groups", "inst"), None),
        P("groups"),
        P("groups"),
        P("groups"),
        P("groups"),
    )
    return jax.shard_map(
        functools.partial(local, mesh.shape["inst"]),
        mesh=mesh,
        in_specs=placed,
        out_specs=(P(("groups", "inst"), None), P(("groups", "inst"), None, None)),
        check_vma=False,
    )
```

profile of v0, /device:TPU:0, one launch (start us, length us, event | category | flops | bytes accessed | tf_op | source)
XLA Modules:
  0.0 127.4 jit_solution(9506391644870231034)
XLA Ops:
  0.6 0.8 select_reduce_fusion.1.refs_2_
  1.4 0.8 select_reduce_fusion.refs_3_
  2.2 0.0 copy-start
  2.2 1.6 %copy-done = bf16[128,8192]{1,0:T(8,128)(2,1)S(1)} copy-done((bf16[128,8192]{1,0:T(8,128)(2,1)S(1)}, bf16[128,8192]{1,0:T(8,128)(2,1)}, u32[]{:S(2)}) %copy-start) | copy-done | bytes 2097176
  3.8 0.0 copy-start.1
  3.8 1.0 copy-done.1
  4.8 0.0 copy-start.2
  4.8 0.7 copy-done.2
  5.5 0.0 copy-start.3
  5.5 0.7 copy-done.3
  6.1 119.1 %shard_map.86 = (bf16[128,8192]{1,0:T(8,128)(2,1)S(1)}, bf16[8,16,2048]{2,1,0:T(8,128)(2,1)S(1)}) custom-call(s32[16]{0:T(128)S(1)} %copy-done.2, s32[16]{0:T(128)S(1)} %copy-done.3, s32[16]{0:T(128)S(1)} %select_reduce_fusion.1.refs_2_, s32[128]{0:T(128)S(1)} %select_reduce_fusion.refs_3_, bf16[128,8192]{1,0:T(8,128)(2,1)S(1)} %copy-done, ...), custom_call_target="tpu_custom_call" | custom-call | tf_op jit(solution)/shard_map/pallas_call | solution.py:289
  125.3 1.3 %copy.11 = bf16[128,8192]{1,0:T(8,128)(2,1)} copy(bf16[128,8192]{1,0:T(8,128)(2,1)S(1)} %get-tuple-element.4) | data formatting | bytes 4194304
  126.6 0.8 copy.12
Async XLA Ops:
  2.2 1.6 %copy-start = (bf16[128,8192]{1,0:T(8,128)(2,1)S(1)}, bf16[128,8192]{1,0:T(8,128)(2,1)}, u32[]{:S(2)}) copy-start(bf16[128,8192]{1,0:T(8,128)(2,1)} %refs_4_.1) | copy-start | bytes 6291460
  3.8 1.0 copy-start.1
  4.8 0.7 copy-start.2
  5.5 0.7 copy-start.3
where the time goes:
time: 128 us; the launch traced here: 127 us
  Pallas kernels  119 us (93%)
  local copies, waits for them, and re-layouts  6.06 us (5%)
  other arithmetic  1.53 us (1%)
    pallas_call x1, Pallas kernels, local(): pl.pallas_call(functools.partial(kernel, n, with_pages), out_shape=out_sh...  119 us
    unnamed x10, local copies, waits for them, and re-layouts  6.06 us

commit v1 on v0

--- a/solution.py
+++ b/solution.py
@@ -16,6 +16,7 @@
 GROUP_WIDTH = HEADS // KV_HEADS * HEAD_DIM
 ROWS = 16
 COLS = 512
+LIMITS = (5, 8)
 MESH = pl.DeviceIdType.MESH
 
 
@@ -254,9 +255,300 @@
     return arrived.reshape(pages_here, PAGE, span_kv.shape[1])
 
 
+def line_kernel(n, most, counts, lengths, source_of, page_source, plan, q_hbm, span_hbm,
+                prefix_hbm, new_hbm, out_hbm, pages_hbm, q, kv, bias, stage, middle, outward,
+                final, page_stage, page_held, *rest):
+    near, far = rest[:KV_HEADS], rest[KV_HEADS:2 * KV_HEADS]
+    (q_sem, k_sem, v_sem, span_sem, near_sem, next_sem, far_sem, page_sem,
+     sent) = rest[2 * KV_HEADS:]
+    me = lax.axis_index("inst")
+    plane, lane = me // 4, me % 4
+    half = me // 8
+    inner = (plane == 1) | (plane == 2)
+    beside = (plane + 1 - 2 * (plane % 2)) * 4 + lane
+    across = (3 - plane) * 4 + lane
+    span = span_hbm.shape[0]
+    prefix = prefix_hbm.shape[0]
+    keys = prefix + span
+    block = span // 4
+    pages_dev = span // PAGE
+
+    span_copy = pltpu.make_async_copy(span_hbm, kv.at[pl.ds(prefix, span)], span_sem)
+    loads = []
+    for g in range(KV_HEADS):
+        wide = pl.ds(g * GROUP_WIDTH, GROUP_WIDTH)
+        k_cols = pl.ds(g * HEAD_DIM, HEAD_DIM)
+        v_cols = pl.ds(KEY_WIDTH + g * HEAD_DIM, HEAD_DIM)
+        loads.append([
+            pltpu.make_async_copy(q_hbm.at[:, wide], q.at[:, wide], q_sem.at[g]),
+            pltpu.make_async_copy(
+                prefix_hbm.at[:, k_cols], kv.at[pl.ds(0, prefix), k_cols], k_sem.at[g]),
+            pltpu.make_async_copy(
+                prefix_hbm.at[:, v_cols], kv.at[pl.ds(0, prefix), v_cols], v_sem.at[g]),
+        ])
+    span_copy.start()
+    for group in loads:
+        for copy in group:
+            copy.start()
+
+    barrier = pltpu.get_barrier_semaphore()
+
+    @pl.loop(1, n)
+    def _(k):
+        pl.semaphore_signal(
+            barrier, inc=1, device_id={"inst": lax.rem(me + k, n)}, device_id_type=MESH)
+
+    count = counts[me]
+    length = lengths[me]
+    row = lax.broadcasted_iota(jnp.int32, (span, keys), 0)
+    column = lax.broadcasted_iota(jnp.int32, (span, keys), 1)
+    limit = jnp.where(column < prefix, length, row + (prefix + 1))
+    bias[...] = jnp.where(column < limit, 0.0, -1e30)
+    pl.semaphore_wait(barrier, n - 1)
+
+    def remote(src, dst, send, recv, peer):
+        return pltpu.make_async_remote_copy(
+            src_ref=src, dst_ref=dst, send_sem=send, recv_sem=recv,
+            device_id={"inst": peer}, device_id_type=MESH)
+
+    def finish(ref, sem):
+        pltpu.make_async_copy(ref, ref, sem).wait()
+
+    own_pages = page_held.at[pl.ds(me * pages_dev, pages_dev)]
+
+    @pl.loop(1, n)
+    def _(k):
+        peer = lax.rem(me + k, n)
+        remote(new_hbm.at[:, :, pl.ds(pl.multiple_of(peer * 128, 128), 128)], own_pages,
+               page_sem.at[0], page_sem.at[1], peer).start()
+
+    pltpu.make_async_copy(
+        new_hbm.at[:, :, pl.ds(pl.multiple_of(me * 128, 128), 128)], own_pages,
+        page_sem.at[1]).start()
+
+    scale = math.log2(math.e) / math.sqrt(HEAD_DIM)
+    live = lax.broadcasted_iota(jnp.int32, (span, HEAD_DIM), 0) < count
+
+    def attend(g):
+        for copy in loads[g]:
+            copy.wait()
+
+        @pl.loop(0, 4)
+        def _(pair):
+            first = pl.multiple_of(g * GROUP_WIDTH + pair * 256, 256)
+            two = q[:, pl.ds(first, 256)]
+            rows = jnp.concatenate([two[:, :HEAD_DIM], two[:, HEAD_DIM:]], axis=0)
+            key = kv[:, g * HEAD_DIM:(g + 1) * HEAD_DIM]
+            value = kv[:, KEY_WIDTH + g * HEAD_DIM:KEY_WIDTH + (g + 1) * HEAD_DIM]
+            scores = lax.dot_general(
+                rows, key, (((1,), (1,)), ((), ())), preferred_element_type=jnp.float32)
+            scores = scores.reshape(2, span, keys) * scale + bias[...][None]
+            top = jnp.max(scores, axis=2, keepdims=True)
+            shifted = jnp.exp2(scores - top)
+            total = jnp.sum(shifted, axis=2, keepdims=True)
+            mixed = jnp.dot(
+                shifted.reshape(2 * span, keys).astype(jnp.bfloat16), value,
+                preferred_element_type=jnp.float32)
+            mixed = mixed.reshape(2, span, HEAD_DIM) / total
+            mixed = jnp.where(live[None], mixed, 0.0).astype(jnp.bfloat16)
+            for h in range(2):
+                at = pl.multiple_of(pair * 256 + h * HEAD_DIM, HEAD_DIM)
+                for r in range(4):
+                    stage[g, r, :, pl.ds(at, HEAD_DIM)] = mixed[h, r * block:(r + 1) * block]
+
+    def spread(g):
+        @pl.loop(1, 4)
+        def _(k):
+            to = lax.rem(lane + k, 4)
+            remote(stage.at[g, to], near[g].at[lane], sent.at[0], near_sem.at[g],
+                   plane * 4 + to).start()
+
+        pltpu.make_async_copy(stage.at[g, lane], near[g].at[lane], near_sem.at[g]).start()
+
+    def to_inner(g):
+        finish(near[g].at[pl.ds(0, 4)], near_sem.at[g])
+
+        @pl.when(jnp.logical_not(inner))
+        def _():
+            remote(near[g].at[pl.ds(0, 4)], near[g].at[pl.ds(4, 4)], sent.at[1],
+                   next_sem.at[g], beside).start()
+
+    def near_place(source):
+        other = jnp.where(inner & (source // 4 != plane), 4, 0)
+        return other + source % 4
+
+    def cross(g):
+        @pl.when(inner)
+        def _():
+            finish(near[g].at[pl.ds(4, 4)], next_sem.at[g])
+
+            @pl.loop(0, most)
+            def _(r):
+                middle[g, r] = near[g][near_place(plan[half * 8 + r])]
+
+            remote(middle.at[g], far[g].at[pl.ds(0, most)], sent.at[2], far_sem.at[g],
+                   across).start()
+
+    def pick(g, dest, k):
+        source = source_of[dest]
+        from_far = jnp.where(inner, source // 8 != half, source // 4 != plane)
+        far_place = jnp.where(inner, plan[16 + source], k)
+        return lax.select_n(from_far, near[g][near_place(source)], far[g][far_place])
+
+    def to_outer(g):
+        @pl.when(inner)
+        def _():
+            finish(far[g].at[pl.ds(0, most)], far_sem.at[g])
+
+            @pl.loop(0, 4)
+            def _(k):
+                outward[g, k] = pick(g, beside - lane + k, k)
+
+            remote(outward.at[g], far[g].at[pl.ds(0, 4)], sent.at[3], far_sem.at[g],
+                   beside).start()
+
+    def deliver(g):
+        @pl.when(jnp.logical_not(inner))
+        def _():
+            finish(far[g].at[pl.ds(0, 4)], far_sem.at[g])
+
+        place = out_hbm.at[
+            pl.ds(pl.multiple_of(lane * block, block), block),
+            pl.ds(g * GROUP_WIDTH, GROUP_WIDTH),
+        ]
+
+        @pl.loop(0, 4)
+        def _(k):
+            to = lax.rem(lane + k, 4)
+            final[g, to] = pick(g, plane * 4 + to, to)
+
+            @pl.when(k > 0)
+            def _():
+                remote(final.at[g, to], place, sent.at[4], sent.at[5], plane * 4 + to).start()
+
+            @pl.when(k == 0)
+            def _():
+                pltpu.make_async_copy(final.at[g, to], place, sent.at[5]).start()
+
+    def send_pages():
+        finish(page_held, page_sem.at[1])
+        place = pages_hbm.at[:, :, pl.ds(pl.multiple_of(me * 128, 128), 128)]
+
+        @pl.loop(0, n)
+        def _(k):
+            peer = lax.rem(me + k, n)
+            for slot in range(pages_dev):
+                at = peer * pages_dev + slot
+                page_stage[at] = page_held[page_source[at]]
+
+            src = page_stage.at[pl.ds(peer * pages_dev, pages_dev)]
+
+            @pl.when(k > 0)
+            def _():
+                remote(src, place, page_sem.at[2], page_sem.at[3], peer).start()
+
+            @pl.when(k == 0)
+            def _():
+                pltpu.make_async_copy(src, place, page_sem.at[3]).start()
+
+    span_copy.wait()
+    steps = [(attend, 0), (spread, 0), (to_inner, 1), (cross, 2), (to_outer, 4), (deliver, 6)]
+    for t in range(KV_HEADS + 6):
+        for step, lag in steps:
+            if 0 <= t - lag < KV_HEADS:
+                step(t - lag)
+        if t == 3:
+            send_pages()
+
+    finish(stage.at[:, pl.ds(0, 3)], sent.at[0])
+
+    @pl.when(inner)
+    def _():
+        finish(middle, sent.at[2])
+        finish(outward, sent.at[3])
+
+    @pl.when(jnp.logical_not(inner))
+    def _():
+        finish(stage, sent.at[1])
+
+    finish(final.at[:, pl.ds(0, 3)], sent.at[4])
+    finish(out_hbm, sent.at[5])
+    finish(page_held.at[pl.ds(0, (n - 1) * pages_dev)], page_sem.at[0])
+    finish(page_stage.at[pl.ds(0, (n - 1) * pages_dev)], page_sem.at[2])
+    finish(pages_hbm, page_sem.at[3])
+
+
+def line_call(n, most, number, small, big):
+    span, width = big[0].shape
+    prefix, kv_width = big[2].shape
+    block = span // 4
+    dma = pltpu.SemaphoreType.DMA
+    bf16 = jnp.bfloat16
+    piece = (block, GROUP_WIDTH)
+    pages = big[3].shape[0] * n
+    return pl.pallas_call(
+        functools.partial(line_kernel, n, most),
+        out_shape=[
+            jax.ShapeDtypeStruct((span, width), bf16),
+            jax.ShapeDtypeStruct(big[3].shape, bf16),
+        ],
+        in_specs=[pl.BlockSpec(memory_space=pltpu.SMEM)] * len(small)
+        + [pl.BlockSpec(memory_space=pl.ANY)] * len(big),
+        out_specs=[pl.BlockSpec(memory_space=pl.ANY)] * 2,
+        scratch_shapes=[
+            pltpu.VMEM((span, width), bf16),
+            pltpu.VMEM((prefix + span, kv_width), bf16),
+            pltpu.VMEM((span, prefix + span), jnp.float32),
+            pltpu.VMEM((KV_HEADS, 4) + piece, bf16),
+            pltpu.VMEM((KV_HEADS, most) + piece, bf16),
+            pltpu.VMEM((KV_HEADS, 4) + piece, bf16),
+            pltpu.VMEM((KV_HEADS, 4) + piece, bf16),
+            pltpu.VMEM((pages, PAGE, 128), bf16),
+            pltpu.VMEM((pages, PAGE, 128), bf16),
+        ]
+        + [pltpu.VMEM((8,) + piece, bf16) for _ in range(KV_HEADS)]
+        + [pltpu.VMEM((max(most, 4),) + piece, bf16) for _ in range(KV_HEADS)]
+        + [
+            dma((KV_HEADS,)), dma((KV_HEADS,)), dma((KV_HEADS,)), dma(()),
+            dma((KV_HEADS,)), dma((KV_HEADS,)), dma((KV_HEADS,)), dma((4,)), dma((6,)),
+        ],
+        compiler_params=pltpu.CompilerParams(
+            collective_id=number, has_side_effects=True, vmem_limit_bytes=48 * 1024 * 1024),
+    )(*small, *big)
+
+
+def by_lines(queries, span_kv, prefix_kv, span_counts, prefix_lengths, move_to, page_slot):
+    n = 16
+    span, kv_width = span_kv.shape
+    index = jnp.arange(n, dtype=jnp.int32)
+    leaves = index // 8 != move_to // 8
+    same_half = index[:, None] // 8 == index[None, :] // 8
+    earlier = same_half & (index[None, :] < index[:, None]) & leaves[None, :]
+    rank = jnp.where(leaves, jnp.sum(earlier.astype(jnp.int32), axis=1), 0)
+    place = jnp.where(leaves, rank + index // 8 * 8, -1)
+    order = jnp.sum(jnp.where(place[None, :] == index[:, None], index[None, :], 0), axis=1)
+    most = jnp.sum(leaves.astype(jnp.int32)) // 2
+    groups = lax.axis_size("groups")
+    for k in range(1, groups):
+        ring = [(g, (g + k) % groups) for g in range(groups)]
+        most = jnp.maximum(most, lax.ppermute(jnp.sum(leaves.astype(jnp.int32)) // 2, "groups", ring))
+    small = [span_counts, prefix_lengths, inverse(move_to), inverse(page_slot),
+             jnp.concatenate([order, rank])]
+    big = [queries, span_kv, prefix_kv, span_kv.reshape(span // PAGE, PAGE, kv_width)]
+    limits = LIMITS
+    branches = [
+        functools.partial(line_call, n, limit, 1 + i) for i, limit in enumerate(limits)
+    ]
+    which = sum([(most > limit).astype(jnp.int32) for limit in limits[:-1]])
+    return tuple(lax.switch(which, branches, small, big))
+
+
 def local(n, queries, span_kv, prefix_kv, span_counts, prefix_lengths, move_to, page_slot):
     span, width = queries.shape
     prefix, kv_width = prefix_kv.shape
+    if n == 16:
+        return by_lines(
+            queries, span_kv, prefix_kv, span_counts, prefix_lengths, move_to, page_slot)
     with_pages = n * 128 == kv_width
     chunks = 128 // n
     anywhere = pl.BlockSpec(memory_space=pl.ANY)

time: 128 us -> 116 us (0.906)
  Pallas kernels: 119 us -> 102 us
  starting transfers between devices: 0 us -> 4.3 us
  local copies, waits for them, and re-layouts: 6.06 us -> 2.14 us
  between operations: 0.66 us -> 3.97 us
  other arithmetic: 1.53 us -> 3.22 us
    pallas_call x1, Pallas kernels: 119 us -> 102 us  [line_call(): pl.pallas_call(functools.partial(line_kernel, n, most), out_shape=[jax.Sh...]
    ppermute x0 -> x1, starting transfers between devices: none -> 4.3 us  [by_lines(): lax.ppermute(jnp.sum(leaves.astype(jnp.int32)) // 2, 'groups', ring)]
    unnamed x10 -> x2, local copies, waits for them, and re-layouts: 6.06 us -> 2.11 us
    reduce_sum x0 -> x3, other arithmetic: none -> 1.6 us  [the longest x1 1.3 us: by_lines(): most = jnp.sum(leaves.astype(jnp.int32)) // 2]
  transfers between devices with their start and end apart: 0 -> 1, of which waited for: 0 -> 0; matrix products, arithmetic and copies ran while one was open for 0% -> 0% of each run, Pallas kernels for 0% -> 0%
where the time goes in v1:
time: 116 us
  Pallas kernels  102 us (88%)
  starting transfers between devices  4.3 us (4%)
  between operations  3.97 us (3%)
  other arithmetic  3.22 us (3%)
  local copies, waits for them, and re-layouts  2.14 us (2%)
    pallas_call x1, Pallas kernels, line_call(): pl.pallas_call(functools.partial(line_kernel, n, most), out_shape=[jax.Sh...  102 us
    ppermute x1, starting transfers between devices, by_lines(): lax.ppermute(jnp.sum(leaves.astype(jnp.int32)) // 2, 'groups', ring)  4.3 us
  transfers between devices with their start and end apart: 1, of which 0 were waited for; matrix products, arithmetic and copies ran while one was open for 0% of the time, Pallas kernels for 0%

profile of v1, /device:TPU:0, one launch (start us, length us, event | category | flops | bytes accessed | tf_op | source)
XLA Modules:
  0.0 115.5 jit_solution(11255371609992943414)
XLA Ops:
  0.6 1.3 %convert_reduce_fusion.1 = (s32[]{:T(128)}, pred[16]{0:T(512)(128)(4,1)S(1)}, s32[16]{0:T(128)S(1)}) fusion(s32[16]{0:T(128)} %param.14), kind=kLoop, calls=%fused_computation.20 | loop fusion | flops 415 | bytes 148 | tf_op jit(solution)/shard_map/reduce_sum | solution.py:530
  4.5 4.3 %collective-permute-start = (s32[]{:T(128)}, s32[]{:T(128)}, u32[]{:S(2)}, u32[]{:S(2)}) collective-permute-start(s32[]{:T(128)} %select_n.55), channel_id=1, source_target_pairs={{0,16},{16,0},{1,17},{17,1},{2,18},{18,2},{3,19},{19,3},{4,20},{20... | collective-permute-start | bytes 20 | tf_op jit(solution)/shard_map/ppermute | solution.py:534
  8.8 0.2 convert_reduce_fusion
  9.0 0.1 select_reduce_fusion.4
  9.1 0.1 pad_add_fusion
  9.3 0.0 collective-permute-done
  10.0 103.4 %conditional.1 = ((bf16[128,8192]{1,0:T(8,128)(2,1)S(1)}, bf16[8,16,2048]{2,1,0:T(8,128)(2,1)S(1)})) conditional(s32[]{:T(128)} %clamp.3, (s32[16]{0:T(128)}, s32[16]{0:T(128)}, s32[16]{0:T(128)}, s32[128]{0:T(128)}, s32[32]{0:T(128)S(1)}, /*index=5*/bf16[128,8192]{1,0:T(8,128)(2,1)}, bf16[128,2048]{1,0:T(8,128)(2,1)}, ...), branch_computations={%region_5.6_spmd.clone, %region_6.7_spmd.clone} | conditional | flops 49776 | bytes 135316 | solution.py:543
  10.0 0.8 select_reduce_fusion.page_source
  10.7 0.8 select_reduce_fusion.1.source_of
  11.5 101.6 %branch_0_fun.1 = (bf16[128,8192]{1,0:T(8,128)(2,1)S(1)}, bf16[8,16,2048]{2,1,0:T(8,128)(2,1)S(1)}) custom-call(s32[16]{0:T(128)} %get-tuple-element.125.counts, s32[16]{0:T(128)} %get-tuple-element.126.lengths, s32[16]{0:T(128)S(1)} %select_reduce_fusion.1.source_of, s32[128]{0:T(128)S(1)} %select_reduce_fusion.page_source, s32[32]{0:T(128)S(1)} %get-tuple-element.118.plan, ...), custom_call_target="tpu_custom_call" | custom-call | tf_op jit(solution)/shard_map/cond/branch_0_fun/pallas_call | solution.py:489
  113.4 1.3 %copy.43 = bf16[128,8192]{1,0:T(8,128)(2,1)} copy(bf16[128,8192]{1,0:T(8,128)(2,1)S(1)} %get-tuple-element.199) | data formatting | bytes 4194304
  114.7 0.8 copy.44
  (6 shorter events, 0.0 us)
Async XLA Ops:
  4.5 4.7 %collective-permute-start = (s32[]{:T(128)}, s32[]{:T(128)}, u32[]{:S(2)}, u32[]{:S(2)}) collective-permute-start(s32[]{:T(128)} %select_n.55), channel_id=1, source_target_pairs={{0,16},{16,0},{1,17},{17,1},{2,18},{18,2},{3,19},{19,3},{4,20},{20... | collective-permute-start | bytes 20 | tf_op jit(solution)/shard_map/ppermute | solution.py:534

commit v2 on v1

--- a/solution.py
+++ b/solution.py
@@ -16,7 +16,9 @@
 GROUP_WIDTH = HEADS // KV_HEADS * HEAD_DIM
 ROWS = 16
 COLS = 512
-LIMITS = (5, 8)
+LIMITS = (4, 5, 8)
+STEPS = 16
+STEP_WIDTH = HEADS * HEAD_DIM // STEPS
 MESH = pl.DeviceIdType.MESH
 
 
@@ -258,9 +260,9 @@
 def line_kernel(n, most, counts, lengths, source_of, page_source, plan, q_hbm, span_hbm,
                 prefix_hbm, new_hbm, out_hbm, pages_hbm, q, kv, bias, stage, middle, outward,
                 final, page_stage, page_held, *rest):
-    near, far = rest[:KV_HEADS], rest[KV_HEADS:2 * KV_HEADS]
+    near, far = rest[:STEPS], rest[STEPS:2 * STEPS]
     (q_sem, k_sem, v_sem, span_sem, near_sem, next_sem, far_sem, page_sem,
-     sent) = rest[2 * KV_HEADS:]
+     sent) = rest[2 * STEPS:]
     me = lax.axis_index("inst")
     plane, lane = me // 4, me % 4
     half = me // 8
@@ -329,13 +331,15 @@
     scale = math.log2(math.e) / math.sqrt(HEAD_DIM)
     live = lax.broadcasted_iota(jnp.int32, (span, HEAD_DIM), 0) < count
 
-    def attend(g):
-        for copy in loads[g]:
-            copy.wait()
-
-        @pl.loop(0, 4)
+    def attend(c):
+        g = c * KV_HEADS // STEPS
+        if c * KV_HEADS % STEPS == 0:
+            for copy in loads[g]:
+                copy.wait()
+
+        @pl.loop(0, STEP_WIDTH // 256)
         def _(pair):
-            first = pl.multiple_of(g * GROUP_WIDTH + pair * 256, 256)
+            first = pl.multiple_of(c * STEP_WIDTH + pair * 256, 256)
             two = q[:, pl.ds(first, 256)]
             rows = jnp.concatenate([two[:, :HEAD_DIM], two[:, HEAD_DIM:]], axis=0)
             key = kv[:, g * HEAD_DIM:(g + 1) * HEAD_DIM]
@@ -354,7 +358,7 @@
             for h in range(2):
                 at = pl.multiple_of(pair * 256 + h * HEAD_DIM, HEAD_DIM)
                 for r in range(4):
-                    stage[g, r, :, pl.ds(at, HEAD_DIM)] = mixed[h, r * block:(r + 1) * block]
+                    stage[c, r, :, pl.ds(at, HEAD_DIM)] = mixed[h, r * block:(r + 1) * block]
 
     def spread(g):
         @pl.loop(1, 4)
@@ -414,7 +418,7 @@
 
         place = out_hbm.at[
             pl.ds(pl.multiple_of(lane * block, block), block),
-            pl.ds(g * GROUP_WIDTH, GROUP_WIDTH),
+            pl.ds(g * STEP_WIDTH, STEP_WIDTH),
         ]
 
         @pl.loop(0, 4)
@@ -452,12 +456,12 @@
                 pltpu.make_async_copy(src, place, page_sem.at[3]).start()
 
     span_copy.wait()
-    steps = [(attend, 0), (spread, 0), (to_inner, 1), (cross, 2), (to_outer, 4), (deliver, 6)]
-    for t in range(KV_HEADS + 6):
+    steps = [(attend, 0), (spread, 0), (to_inner, 1), (cross, 3), (to_outer, 6), (deliver, 8)]
+    for t in range(STEPS + 8):
         for step, lag in steps:
-            if 0 <= t - lag < KV_HEADS:
+            if 0 <= t - lag < STEPS:
                 step(t - lag)
-        if t == 3:
+        if t == 5:
             send_pages()
 
     finish(stage.at[:, pl.ds(0, 3)], sent.at[0])
@@ -484,7 +488,7 @@
     block = span // 4
     dma = pltpu.SemaphoreType.DMA
     bf16 = jnp.bfloat16
-    piece = (block, GROUP_WIDTH)
+    piece = (block, STEP_WIDTH)
     pages = big[3].shape[0] * n
     return pl.pallas_call(
         functools.partial(line_kernel, n, most),
@@ -499,18 +503,18 @@
             pltpu.VMEM((span, width), bf16),
             pltpu.VMEM((prefix + span, kv_width), bf16),
             pltpu.VMEM((span, prefix + span), jnp.float32),
-            pltpu.VMEM((KV_HEADS, 4) + piece, bf16),
-            pltpu.VMEM((KV_HEADS, most) + piece, bf16),
-            pltpu.VMEM((KV_HEADS, 4) + piece, bf16),
-            pltpu.VMEM((KV_HEADS, 4) + piece, bf16),
+            pltpu.VMEM((STEPS, 4) + piece, bf16),
+            pltpu.VMEM((STEPS, most) + piece, bf16),
+            pltpu.VMEM((STEPS, 4) + piece, bf16),
+            pltpu.VMEM((STEPS, 4) + piece, bf16),
             pltpu.VMEM((pages, PAGE, 128), bf16),
             pltpu.VMEM((pages, PAGE, 128), bf16),
         ]
-        + [pltpu.VMEM((8,) + piece, bf16) for _ in range(KV_HEADS)]
-        + [pltpu.VMEM((max(most, 4),) + piece, bf16) for _ in range(KV_HEADS)]
+        + [pltpu.VMEM((8,) + piece, bf16) for _ in range(STEPS)]
+        + [pltpu.VMEM((max(most, 4),) + piece, bf16) for _ in range(STEPS)]
         + [
             dma((KV_HEADS,)), dma((KV_HEADS,)), dma((KV_HEADS,)), dma(()),
-            dma((KV_HEADS,)), dma((KV_HEADS,)), dma((KV_HEADS,)), dma((4,)), dma((6,)),
+            dma((STEPS,)), dma((STEPS,)), dma((STEPS,)), dma((4,)), dma((6,)),
         ],
         compiler_params=pltpu.CompilerParams(
             collective_id=number, has_side_effects=True, vmem_limit_bytes=48 * 1024 * 1024),

time: 116 us -> 102 us (0.88)
  Pallas kernels: 102 us -> 87.6 us
    pallas_call x1, Pallas kernels: 102 us -> 87.6 us  [line_call(): pl.pallas_call(functools.partial(line_kernel, n, most), out_shape=[jax.Sh...]
where the time goes in v2:
time: 102 us
  Pallas kernels  87.6 us (86%)
  starting transfers between devices  4.3 us (4%)
  between operations  3.97 us (4%)
  other arithmetic  3.22 us (3%)
  local copies, waits for them, and re-layouts  2.14 us (2%)
    pallas_call x1, Pallas kernels, line_call(): pl.pallas_call(functools.partial(line_kernel, n, most), out_shape=[jax.Sh...  87.6 us
    ppermute x1, starting transfers between devices, by_lines(): lax.ppermute(jnp.sum(leaves.astype(jnp.int32)) // 2, 'groups', ring)  4.3 us
    unnamed x2, local copies, waits for them, and re-layouts  2.11 us
  transfers between devices with their start and end apart: 1, of which 0 were waited for; matrix products, arithmetic and copies ran while one was open for 0% of the time, Pallas kernels for 0%

profile of v2, /device:TPU:0, one launch (start us, length us, event | category | flops | bytes accessed | tf_op | source)
XLA Modules:
  0.0 101.8 jit_solution(2484295683862292849)
XLA Ops:
  0.6 1.3 %convert_reduce_fusion.1 = (s32[]{:T(128)}, pred[16]{0:T(512)(128)(4,1)S(1)}, s32[16]{0:T(128)S(1)}) fusion(s32[16]{0:T(128)} %param.15), kind=kLoop, calls=%fused_computation.22 | loop fusion | flops 415 | bytes 148 | tf_op jit(solution)/shard_map/reduce_sum | solution.py:534
  4.5 4.3 %collective-permute-start = (s32[]{:T(128)}, s32[]{:T(128)}, u32[]{:S(2)}, u32[]{:S(2)}) collective-permute-start(s32[]{:T(128)} %select_n.55), channel_id=1, source_target_pairs={{0,16},{16,0},{1,17},{17,1},{2,18},{18,2},{3,19},{19,3},{4,20},{20... | collective-permute-start | bytes 20 | tf_op jit(solution)/shard_map/ppermute | solution.py:538
  8.8 0.2 convert_reduce_fusion
  9.0 0.1 select_reduce_fusion.6
  9.1 0.1 pad_add_fusion
  9.3 0.0 collective-permute-done
  10.0 89.7 %conditional.1 = ((bf16[128,8192]{1,0:T(8,128)(2,1)S(1)}, bf16[8,16,2048]{2,1,0:T(8,128)(2,1)S(1)})) conditional(s32[]{:T(128)} %clamp.3, (s32[16]{0:T(128)}, s32[16]{0:T(128)}, s32[16]{0:T(128)}, s32[128]{0:T(128)}, s32[32]{0:T(128)S(1)}, /*index=5*/bf16[128,8192]{1,0:T(8,128)(2,1)}, bf16[128,2048]{1,0:T(8,128)(2,1)}, ...), branch_computations={%region_5.6_spmd.clone, %region_6.7_spmd.clone, %region_7.8_spmd.c... | conditional | flops 49776 | bytes 135316 | solution.py:547
  10.0 0.8 select_reduce_fusion.page_source
  10.7 0.8 select_reduce_fusion.1.source_of
  11.5 87.6 %branch_0_fun.1 = (bf16[128,8192]{1,0:T(8,128)(2,1)S(1)}, bf16[8,16,2048]{2,1,0:T(8,128)(2,1)S(1)}) custom-call(s32[16]{0:T(128)} %get-tuple-element.182.counts, s32[16]{0:T(128)} %get-tuple-element.183.lengths, s32[16]{0:T(128)S(1)} %select_reduce_fusion.1.source_of, s32[128]{0:T(128)S(1)} %select_reduce_fusion.page_source, s32[32]{0:T(128)S(1)} %get-tuple-element.175.plan, ...), custom_call_target="tpu_custom_call" | custom-call | tf_op jit(solution)/shard_map/cond/branch_0_fun/pallas_call | solution.py:493
  99.7 1.3 %copy.59 = bf16[128,8192]{1,0:T(8,128)(2,1)} copy(bf16[128,8192]{1,0:T(8,128)(2,1)S(1)} %get-tuple-element.293) | data formatting | bytes 4194304
  101.0 0.8 copy.60
  (6 shorter events, 0.0 us)
Async XLA Ops:
  4.5 4.7 %collective-permute-start = (s32[]{:T(128)}, s32[]{:T(128)}, u32[]{:S(2)}, u32[]{:S(2)}) collective-permute-start(s32[]{:T(128)} %select_n.55), channel_id=1, source_target_pairs={{0,16},{16,0},{1,17},{17,1},{2,18},{18,2},{3,19},{19,3},{4,20},{20... | collective-permute-start | bytes 20 | tf_op jit(solution)/shard_map/ppermute | solution.py:538
